TPU v7x, 32 devices: a whole 2x2x4 slice. The times are simulated.
32 devices in a mesh: dp: 8 (over y, x, core), tensor: 4 (over z).
Axes of the slice: x: 2, y: 2, z: 4, core: 2. Of those that a mesh axis runs over, the one named last changes fastest.
Arguments:
- block_input: bfloat16 [8192, 768], P(('dp', 'tensor')), may hold values from -6 to 6
- doc_lengths: int32 [8, 2], P('dp'), may hold values from 0 to 1024, as said below
- first_gain: bfloat16 [768], P(('dp', 'tensor')), may hold values from 0.5 to 1.5
- first_shift: bfloat16 [768], P(('dp', 'tensor')), may hold values from -1 to 1
- qkv_weight: bfloat16 [768, 3, 768], P('dp', None, 'tensor'), may hold values from -0.21875 to 0.21875
- attn_bias: bfloat16 [1536], P(('dp', 'tensor')), may hold values from -1.5 to 1.5
- out_weight: bfloat16 [768, 768], P('tensor', 'dp'), may hold values from -3.5 to 3.5
- out_bias: bfloat16 [768], P(('dp', 'tensor')), may hold values from -1.5 to 1.5
- second_gain: bfloat16 [768], P(('dp', 'tensor')), may hold values from 0.5 to 1.5
- second_shift: bfloat16 [768], P(('dp', 'tensor')), may hold values from -1 to 1
- fc_weight: bfloat16 [768, 3072], P('dp', 'tensor'), may hold values from -0.21875 to 0.21875
- fc_bias: bfloat16 [3072], P(('dp', 'tensor')), may hold values from -1.5 to 1.5
- proj_weight: bfloat16 [3072, 768], P('tensor', 'dp'), may hold values from -0.109375 to 0.109375
- proj_bias: bfloat16 [768], P(('dp', 'tensor')), may hold values from -1.5 to 1.5
- block_grad: bfloat16 [8192, 768], P(('dp', 'tensor')), may hold values from -6 to 6
Outputs:
- block_out: bfloat16 [8192, 768], P(('dp', 'tensor'))
- input_grad: float32 [8192, 768], P(('dp', 'tensor'))
- first_gain_grad: float32 [768], P(('dp', 'tensor'))
- first_shift_grad: float32 [768], P(('dp', 'tensor'))
- qkv_weight_grad: float32 [768, 3, 768], P('dp', None, 'tensor')
- attn_bias_grad: float32 [1536], P(('dp', 'tensor'))
- out_weight_grad: float32 [768, 768], P('tensor', 'dp')
- out_bias_grad: float32 [768], P(('dp', 'tensor'))
- second_gain_grad: float32 [768], P(('dp', 'tensor'))
- second_shift_grad: float32 [768], P(('dp', 'tensor'))
- fc_weight_grad: float32 [768, 3072], P('dp', 'tensor')
- fc_bias_grad: float32 [3072], P(('dp', 'tensor'))
- proj_weight_grad: float32 [3072, 768], P('tensor', 'dp')
- proj_bias_grad: float32 [768], P(('dp', 'tensor'))
Inputs may be any that keep to these rules, and one draw needn't show every extreme that they name: `doc_lengths`: each row holds the lengths of its group's two documents in order; they sum to 1024, and one of them is longer than 768.
All inputs are finite; a program needn't handle non-finite values.
Results may differ from a plain program's by a relative error of at most 0.019.
Values may be sent and summed in bfloat16 or wider, within the bound.
No kernel may reach another device: no remote copies, remote signals or barrier semaphores. Data moves between devices by JAX's collectives and lax.ppermute only.
A program may use at most 128 MiB of HBM per device.

v0:
```python
import jax
import jax.numpy as jnp
from jax import lax
from jax.sharding import PartitionSpec as P

HEAD_DIM = 64
EPS = 1e-05


def in_blocks(shard, dim, size):
    before, after = (shard.shape[:dim], shard.shape[dim + 1 :])
    return jnp.moveaxis(shard.reshape(*before, size, -1, *after), dim, 0)


def sum_at_owner(shard, axis, dim):
    blocks = in_blocks(shard, dim, lax.axis_size(axis))
    arrived = lax.all_to_all(blocks, axis, split_axis=0, concat_axis=0, tiled=True)
    return arrived.astype(jnp.float32).sum(axis=0)


def norm_rows(values, gain_vec, shift_vec):
    center = jnp.mean(values, axis=-1, keepdims=True)
    offset = values - center
    spread = lax.rsqrt(jnp.mean(offset * offset, axis=-1, keepdims=True) + EPS)
    unit_rows = offset * spread
    return (unit_rows * gain_vec + shift_vec, unit_rows, spread)


def norm_back(grad_out, unit_rows, spread, gain_vec):
    scaled = grad_out * gain_vec
    centred = scaled - jnp.mean(scaled, axis=-1, keepdims=True)
    centred = centred - unit_rows * jnp.mean(scaled * unit_rows, axis=-1, keepdims=True)
    return (spread * centred, jnp.sum(grad_out * unit_rows, axis=0), jnp.sum(grad_out, axis=0))


def gelu_tanh(values):
    return jax.nn.gelu(values, approximate=True)


def fetch_attention(qkv_weight, out_weight):
    return (
        lax.all_gather(qkv_weight, "dp", axis=0, tiled=True),
        lax.all_gather(out_weight, "dp", axis=1, tiled=True),
    )


def gather_ffn(fc_weight, proj_weight):
    return (
        lax.all_gather(fc_weight, "dp", axis=0, tiled=True),
        lax.all_gather(proj_weight, "dp", axis=1, tiled=True),
    )


def scatter_ffn(fc_grad, proj_grad):
    fc_grad, proj_grad = (
        lax.psum_scatter(fc_grad, "dp", scatter_dimension=0, tiled=True),
        lax.psum_scatter(proj_grad, "dp", scatter_dimension=1, tiled=True),
    )
    return (fc_grad, proj_grad)


def rows_forward(values):
    return lax.all_gather(values, "tensor", axis=0, tiled=True)


def sums_forward(values):
    return lax.psum_scatter(
        values.astype(jnp.bfloat16), "tensor", scatter_dimension=0, tiled=True
    ).astype(jnp.float32)


def rows_backward(values):
    return lax.all_gather(values, "tensor", axis=0, tiled=True)


def sums_backward(values):
    return lax.psum_scatter(
        values.astype(jnp.bfloat16), "tensor", scatter_dimension=0, tiled=True
    ).astype(jnp.float32)


def score_block(query_block, key_heads, block_start, boundary, score_scale):
    block_rows = query_block.shape[0]
    key_pos = jnp.arange(key_heads.shape[0])
    query_pos = block_start + jnp.arange(block_rows)
    allowed = (key_pos[None, :] <= query_pos[:, None]) & (
        (key_pos[None, :] >= boundary) == (query_pos[:, None] >= boundary)
    )
    scores = (
        jnp.einsum("ihd,jhd->hij", query_block, key_heads, preferred_element_type=jnp.float32)
        * score_scale
    )
    return jnp.where(allowed[None], scores, -jnp.inf)


def attend(query_heads, key_heads, value_heads, boundary, score_scale):
    row_count, heads_dev, head_dim = query_heads.shape
    block_rows = min(512, row_count)
    outputs = []
    totals = []
    for block_start in range(0, row_count, block_rows):
        scores = score_block(
            query_heads[block_start : block_start + block_rows],
            key_heads,
            block_start,
            boundary,
            score_scale,
        )
        row_peak = jnp.max(scores, axis=-1, keepdims=True)
        log_total = row_peak + jnp.log(jnp.sum(jnp.exp(scores - row_peak), axis=-1, keepdims=True))
        probs_low = jnp.exp(scores - log_total).astype(jnp.bfloat16)
        mixed_block = jnp.einsum(
            "hij,jhd->ihd", probs_low, value_heads, preferred_element_type=jnp.float32
        )
        outputs.append(mixed_block.reshape(block_rows, heads_dev * head_dim).astype(jnp.bfloat16))
        totals.append(log_total)
    return (jnp.concatenate(outputs, axis=0), totals)


def attend_back(query_heads, key_heads, value_heads, totals, grad_heads, boundary, score_scale):
    row_count = query_heads.shape[0]
    block_rows = min(512, row_count)
    query_grads = []
    key_acc = jnp.zeros(key_heads.shape, jnp.float32)
    value_acc = jnp.zeros(value_heads.shape, jnp.float32)
    for block_index, block_start in enumerate(range(0, row_count, block_rows)):
        query_block = query_heads[block_start : block_start + block_rows]
        grad_block = grad_heads[block_start : block_start + block_rows]
        scores = score_block(query_block, key_heads, block_start, boundary, score_scale)
        probs = jnp.exp(scores - totals[block_index])
        probs_low = probs.astype(jnp.bfloat16)
        prob_grads = jnp.einsum(
            "ihd,jhd->hij", grad_block, value_heads, preferred_element_type=jnp.float32
        )
        row_dot = jnp.sum(probs * prob_grads, axis=-1, keepdims=True)
        score_grads = (probs * (prob_grads - row_dot)).astype(jnp.bfloat16)
        query_grads.append(
            jnp.einsum("hij,jhd->ihd", score_grads, key_heads, preferred_element_type=jnp.float32)
            * score_scale
        )
        key_acc = key_acc + jnp.einsum(
            "hij,ihd->jhd", score_grads, query_block, preferred_element_type=jnp.float32
        )
        value_acc = value_acc + jnp.einsum(
            "hij,ihd->jhd", probs_low, grad_block, preferred_element_type=jnp.float32
        )
    return (jnp.concatenate(query_grads, axis=0), key_acc * score_scale, value_acc)


def body(
    block_input,
    doc_lengths,
    first_gain,
    first_shift,
    qkv_weight,
    attn_bias,
    out_weight,
    out_bias,
    second_gain,
    second_shift,
    fc_weight,
    fc_bias,
    proj_weight,
    proj_bias,
    block_grad,
):
    small_params = (
        lax.all_gather(first_gain, ("dp", "tensor"), axis=0, tiled=True),
        lax.all_gather(first_shift, ("dp", "tensor"), axis=0, tiled=True),
        lax.all_gather(attn_bias, ("dp", "tensor"), axis=0, tiled=True),
        lax.all_gather(out_bias, ("dp", "tensor"), axis=0, tiled=True),
        lax.all_gather(second_gain, ("dp", "tensor"), axis=0, tiled=True),
        lax.all_gather(second_shift, ("dp", "tensor"), axis=0, tiled=True),
        lax.all_gather(fc_bias, ("dp", "tensor"), axis=0, tiled=True),
        lax.all_gather(proj_bias, ("dp", "tensor"), axis=0, tiled=True),
    )
    gain_one, shift_one, attn_shift, out_shift, gain_two, shift_two, fc_shift, proj_shift = tuple(
        (param.astype(jnp.float32) for param in small_params)
    )
    tensor_rank = lax.axis_index("tensor")
    width = block_input.shape[1]
    width_dev = qkv_weight.shape[2]
    head_dim = HEAD_DIM
    heads_dev = width_dev // head_dim
    score_scale = head_dim ** (-0.5)
    boundary = doc_lengths[0, 0]
    qkv_full, out_full = fetch_attention(qkv_weight, out_weight)
    inputs = block_input.astype(jnp.float32)
    normed_one, unit_one, spread_one = norm_rows(inputs, gain_one, shift_one)
    rows_one = rows_forward(normed_one.astype(jnp.bfloat16))
    row_count = rows_one.shape[0]
    projected = jnp.einsum("ic,cpd->ipd", rows_one, qkv_full, preferred_element_type=jnp.float32)
    query_shift = lax.dynamic_slice_in_dim(attn_shift, tensor_rank * width_dev, width_dev)
    value_shift = lax.dynamic_slice_in_dim(attn_shift, width + tensor_rank * width_dev, width_dev)
    head_shape = (row_count, heads_dev, head_dim)
    queries = (projected[:, 0] + query_shift).astype(jnp.bfloat16).reshape(head_shape)
    key_rows = projected[:, 1].astype(jnp.bfloat16).reshape(head_shape)
    value_rows = (projected[:, 2] + value_shift).astype(jnp.bfloat16).reshape(head_shape)
    mixed_heads, totals = attend(queries, key_rows, value_rows, boundary, score_scale)
    attn_part = jnp.dot(mixed_heads, out_full, preferred_element_type=jnp.float32)
    hidden = inputs + (sums_forward(attn_part) + out_shift)
    normed_two, unit_two, spread_two = norm_rows(hidden, gain_two, shift_two)
    normed_two = normed_two.astype(jnp.bfloat16)
    fc_full, proj_full = gather_ffn(fc_weight, proj_weight)
    hidden_dev = fc_full.shape[1]
    rows_two = rows_forward(normed_two)
    fc_slice = lax.dynamic_slice_in_dim(fc_shift, tensor_rank * hidden_dev, hidden_dev)
    pre_act = jnp.dot(rows_two, fc_full, preferred_element_type=jnp.float32) + fc_slice
    gelu_values, gelu_pull = jax.vjp(gelu_tanh, pre_act)
    activated = gelu_values.astype(jnp.bfloat16)
    mlp_part = jnp.dot(activated, proj_full, preferred_element_type=jnp.float32)
    mlp_out = sums_forward(mlp_part) + proj_shift
    block_out = (hidden + mlp_out).astype(jnp.bfloat16)
    top_grad = block_grad.astype(jnp.float32)
    proj_bias_grad = jnp.sum(top_grad, axis=0)
    fc_back, proj_back = gather_ffn(fc_weight, proj_weight)
    rows_grad = rows_backward(block_grad)
    proj_grad = jnp.einsum("if,id->fd", activated, rows_grad, preferred_element_type=jnp.float32)
    act_grad = jnp.einsum("id,fd->if", rows_grad, proj_back, preferred_element_type=jnp.float32)
    pre_grad = gelu_pull(act_grad)[0].astype(jnp.bfloat16)
    fc_grad = jnp.einsum("ic,if->cf", rows_two, pre_grad, preferred_element_type=jnp.float32)
    fc_cols = jnp.sum(pre_grad.astype(jnp.float32), axis=0)
    normed_two_grad = jnp.einsum("if,cf->ic", pre_grad, fc_back, preferred_element_type=jnp.float32)
    normed_two_grad = sums_backward(normed_two_grad)
    fc_bias_grad = lax.dynamic_update_slice_in_dim(
        jnp.zeros((fc_shift.shape[0],), jnp.float32), fc_cols, tensor_rank * hidden_dev, 0
    )
    fc_weight_grad, proj_weight_grad = scatter_ffn(fc_grad, proj_grad)
    hidden_part, second_gain_grad, second_shift_grad = norm_back(
        normed_two_grad, unit_two, spread_two, gain_two
    )
    hidden_grad = top_grad + hidden_part
    attn_grad = hidden_grad.astype(jnp.bfloat16)
    out_bias_grad = jnp.sum(attn_grad.astype(jnp.float32), axis=0)
    rows_attn = rows_backward(attn_grad)
    qkv_back, out_back = fetch_attention(qkv_weight, out_weight)
    out_grad = jnp.einsum("ik,id->kd", mixed_heads, rows_attn, preferred_element_type=jnp.float32)
    heads_grad = jnp.einsum(
        "id,kd->ik", rows_attn, out_back, preferred_element_type=jnp.float32
    ).astype(jnp.bfloat16)
    query_grad, key_grad, value_grad = attend_back(
        queries, key_rows, value_rows, totals, heads_grad.reshape(head_shape), boundary, score_scale
    )
    flat_shape = (row_count, width_dev)
    query_low = query_grad.reshape(flat_shape).astype(jnp.bfloat16)
    value_low = value_grad.reshape(flat_shape).astype(jnp.bfloat16)
    projection_grads = jnp.stack(
        [query_low, key_grad.reshape(flat_shape).astype(jnp.bfloat16), value_low], axis=1
    )
    qkv_grad = jnp.einsum(
        "ic,ipd->cpd", rows_one, projection_grads, preferred_element_type=jnp.float32
    )
    normed_one_grad = jnp.einsum(
        "ipd,cpd->ic", projection_grads, qkv_back, preferred_element_type=jnp.float32
    )
    normed_one_grad = sums_backward(normed_one_grad)
    attn_bias_grad = jnp.zeros((2 * width,), jnp.float32)
    attn_bias_grad = lax.dynamic_update_slice_in_dim(
        attn_bias_grad, jnp.sum(query_low.astype(jnp.float32), axis=0), tensor_rank * width_dev, 0
    )
    attn_bias_grad = lax.dynamic_update_slice_in_dim(
        attn_bias_grad,
        jnp.sum(value_low.astype(jnp.float32), axis=0),
        width + tensor_rank * width_dev,
        0,
    )
    qkv_weight_grad, out_weight_grad = (
        sum_at_owner(qkv_grad.astype(jnp.bfloat16), "dp", 0),
        sum_at_owner(out_grad.astype(jnp.bfloat16), "dp", 1),
    )
    input_part, first_gain_grad, first_shift_grad = norm_back(
        normed_one_grad, unit_one, spread_one, gain_one
    )
    input_grad = hidden_grad + input_part
    (
        first_gain_grad,
        first_shift_grad,
        attn_bias_grad,
        out_bias_grad,
        second_gain_grad,
        second_shift_grad,
        fc_bias_grad,
        proj_bias_grad,
    ) = (
        lax.psum_scatter(first_gain_grad, ("dp", "tensor"), scatter_dimension=0, tiled=True),
        lax.psum_scatter(first_shift_grad, ("dp", "tensor"), scatter_dimension=0, tiled=True),
        lax.psum_scatter(attn_bias_grad, ("dp", "tensor"), scatter_dimension=0, tiled=True),
        lax.psum_scatter(out_bias_grad, ("dp", "tensor"), scatter_dimension=0, tiled=True),
        lax.psum_scatter(second_gain_grad, ("dp", "tensor"), scatter_dimension=0, tiled=True),
        lax.psum_scatter(second_shift_grad, ("dp", "tensor"), scatter_dimension=0, tiled=True),
        lax.psum_scatter(fc_bias_grad, ("dp", "tensor"), scatter_dimension=0, tiled=True),
        lax.psum_scatter(proj_bias_grad, ("dp", "tensor"), scatter_dimension=0, tiled=True),
    )
    return (
        block_out,
        input_grad,
        first_gain_grad,
        first_shift_grad,
        qkv_weight_grad,
        attn_bias_grad,
        out_weight_grad,
        out_bias_grad,
        second_gain_grad,
        second_shift_grad,
        fc_weight_grad,
        fc_bias_grad,
        proj_weight_grad,
        proj_bias_grad,
    )


def solution(mesh):
    return jax.shard_map(
        body,
        mesh=mesh,
        in_specs=(
            P(("dp", "tensor"), None),
            P("dp", None),
            P(("dp", "tensor")),
            P(("dp", "tensor")),
            P("dp", None, "tensor"),
            P(("dp", "tensor")),
            P("tensor", "dp"),
            P(("dp", "tensor")),
            P(("dp", "tensor")),
            P(("dp", "tensor")),
            P("dp", "tensor"),
            P(("dp", "tensor")),
            P("tensor", "dp"),
            P(("dp", "tensor")),
            P(("dp", "tensor"), None),
        ),
        out_specs=(
            P(("dp", "tensor"), None),
            P(("dp", "tensor"), None),
            P(("dp", "tensor")),
            P(("dp", "tensor")),
            P("dp", None, "tensor"),
            P(("dp", "tensor")),
            P("tensor", "dp"),
            P(("dp", "tensor")),
            P(("dp", "tensor")),
            P(("dp", "tensor")),
            P("dp", "tensor"),
            P(("dp", "tensor")),
            P("tensor", "dp"),
            P(("dp", "tensor")),
        ),
        check_vma=False,
    )
```

profile of v0, /device:TPU:0, one launch (start us, length us, event | category | flops | bytes accessed | tf_op | source)
XLA Modules:
  0.0 531.3 jit_solution(13650693505043165008)
XLA Ops:
  17.2 42.4 %all-reduce.17 = (bf16[1536]{0:T(1024)(128)(2,1)S(1)}, bf16[768]{0:T(1024)(128)(2,1)S(1)}, bf16[768]{0:T(1024)(128)(2,1)S(1)}, bf16[768]{0:T(1024)(128)(2,1)S(1)...) all-reduce(bf16[1536]{0:T(1024)(128)(2,1)S(1)} %dynamic-update-slic, ...), channel_id=1, replica_groups=mesh['dp'=8,'tensor'=4] {'dp','tensor'}, use_global_device_ids=true, to_apply=%add.2 | all-reduce | flops 9216 | bytes 36864
  63.8 12.9 %all_gather.55 = bf16[768,3,192]{2,1,0:T(4,128)(2,1)S(1)} all-gather(bf16[96,3,192]{2,1,0:T(4,128)(2,1)S(1)} %copy.31), channel_id=1, replica_groups=mesh['dp'=8,'tensor'=4] {'dp'}, dimensions={0}, use_global_device_ids=true | all-gather | bytes 995328 | tf_op jit(solution)/shard_map/all_gather | solution.py:42
  77.5 10.3 %all_gather.57 = bf16[192,768]{0,1:T(8,128)(2,1)S(1)} all-gather(bf16[192,96]{0,1:T(8,128)(2,1)S(1)} %copy.33), channel_id=1, replica_groups=mesh['dp'=8,'tensor'=4] {'dp'}, dimensions={1}, use_global_device_ids=true | all-gather | bytes 331776 | tf_op jit(solution)/shard_map/all_gather | solution.py:43
  89.1 9.6 %all-gather.7.cloned.1.call-done = bf16[1024,768]{1,0:T(8,128)(2,1)} async-done(((bf16[256,768]{1,0:T(8,128)(2,1)}), bf16[1024,768]{1,0:T(8,128)(2,1)}) %all-gather.7.cloned.1.call-update) | async-done | bytes 1572880 | tf_op jit(solution)/shard_map/all_gather | solution.py:63
  98.7 2.5 fusion.55
  114.8 33.6 %reduce-scatter.7.cloned.1.call-done = bf16[256,768]{1,0:T(8,128)(2,1)} async-done(((bf16[1024,768]{1,0:T(8,128)(2,1)}), bf16[256,768]{1,0:T(8,128)(2,1)}) %reduce-scatter.7.cloned.1.call-update) | async-done | bytes 393232 | tf_op jit(solution)/shard_map/reduce_scatter | solution.py:67
  154.6 34.4 %all-gather.9.cloned.1.call-done = bf16[1024,768]{1,0:T(8,128)(2,1)} async-done(((bf16[256,768]{1,0:T(8,128)(2,1)}), bf16[1024,768]{1,0:T(8,128)(2,1)}) %all-gather.9.cloned.1.call-update) | async-done | bytes 1572880 | tf_op jit(solution)/shard_map/all_gather | solution.py:63
  189.0 4.8 fusion.56
  193.8 19.7 %all-gather.13.cloned.1.call-done = bf16[768,768]{0,1:T(8,128)(2,1)} async-done(((bf16[768,96]{0,1:T(8,128)(2,1)}), bf16[768,768]{0,1:T(8,128)(2,1)}) %all-gather.13.cloned.1.call-update) | async-done | bytes 1179664 | tf_op jit(solution)/shard_map/all_gather | solution.py:50
  213.5 38.5 %all-gather.15.cloned.1.call-done = bf16[1024,768]{1,0:T(8,128)(2,1)} async-done(((bf16[256,768]{1,0:T(8,128)(2,1)}), bf16[1024,768]{1,0:T(8,128)(2,1)}) %all-gather.15.cloned.1.call-update) | async-done | bytes 1572880 | tf_op jit(solution)/shard_map/all_gather | solution.py:73
  252.0 6.4 %convert_reduce_fusion = (f32[768]{0:T(1024)}, bf16[1024,768]{1,0:T(8,128)(2,1)S(1)}) fusion(f32[1024,768]{1,0:T(8,128)} %fusion.56, f32[768]{0:T(1024)S(1)} %dynamic-slice_convert_fusion, bf16[1024,768]{1,0:T(8,128)(2,1)} %all-gather.15.cloned.1.call-done, bf16[768,768]{0,1:T(8,128)(2,1)} %all-gather.13.cloned.1.call-done), kind=kOutput, calls=%fused_computation.24 | convolution fusion | flops 1226046720 | bytes 7477248 | tf_op jit(solution)/shard_map/id,fd->if/dot_general | solution.py:219
  259.6 2.6 convolution_convert_fusion
  262.3 5.6 %convolution_convert_fusion.1 = bf16[1024,768]{1,0:T(8,128)(2,1)} fusion(bf16[768,768]{0,1:T(8,128)(2,1)} %all-gather.13.cloned.1.call-done, f32[1024,768]{1,0:T(8,128)} %fusion.56, f32[768]{0:T(1024)S(1)} %dynamic-slice_convert_fusion), kind=kOutput, calls=%fused_computation.32 | convolution fusion | flops 1216610304 | bytes 5901312 | tf_op jit(solution)/shard_map/dot_general | solution.py:211
  267.9 28.6 %reduce-scatter.11.cloned.1.call-done = bf16[256,768]{1,0:T(8,128)(2,1)} async-done(((bf16[1024,768]{1,0:T(8,128)(2,1)}), bf16[256,768]{1,0:T(8,128)(2,1)}) %reduce-scatter.11.cloned.1.call-update) | async-done | bytes 393232 | tf_op jit(solution)/shard_map/reduce_scatter | solution.py:77
  298.6 34.3 %reduce-scatter.9.cloned.1.call-done = bf16[256,768]{1,0:T(8,128)(2,1)} async-done(((bf16[1024,768]{1,0:T(8,128)(2,1)}), bf16[256,768]{1,0:T(8,128)(2,1)}) %reduce-scatter.9.cloned.1.call-update) | async-done | bytes 393232 | tf_op jit(solution)/shard_map/reduce_scatter | solution.py:67
  332.9 3.5 convert_reduce_fusion.6
  336.5 36.0 %all-gather.17.cloned.1.call-done = bf16[1024,768]{1,0:T(8,128)(2,1)} async-done(((bf16[256,768]{1,0:T(8,128)(2,1)}), bf16[1024,768]{1,0:T(8,128)(2,1)}) %all-gather.17.cloned.1.call-update) | async-done | bytes 1572880 | tf_op jit(solution)/shard_map/all_gather | solution.py:73
  372.5 2.2 convolution_convert_fusion.3
  374.8 4.7 fusion.47
  379.5 2.5 multiply_reduce_fusion.1
  385.9 2.5 multiply_reduce_fusion
  388.4 2.6 convert_reduce_fusion.8
  395.1 2.6 bitcast_convert_fusion
  397.8 5.1 fusion.50
  403.3 4.9 fusion.58
  411.0 3.7 all-to-all-start.1
  414.8 2.5 fusion.59
  420.0 3.0 all-to-all-done.1
  423.0 3.6 all-to-all-start
  428.2 15.1 %all-to-all-done = bf16[8,96,3,192]{1,3,2,0:T(8,128)(2,1)S(1)} async-done(((bf16[8,96,3,192]{1,3,2,0:T(8,128)(2,1)}), bf16[8,96,3,192]{1,3,2,0:T(8,128)(2,1)S(1)}, u32[]{:S(2)}, u32[]{:S(2)}) %all-to-all-start) | async-done | bytes 884768 | tf_op jit(solution)/shard_map/all_to_all | solution.py:17
  445.9 39.5 %all-reduce.16 = (f32[768]{0:T(1024)S(1)}, f32[768]{0:T(1024)S(1)}, f32[1536]{0:T(1024)S(1)}, f32[768]{0:T(1024)S(1)}, f32[768]{0:T(1024)S(1)}, /*index=5*/f32[7...) all-reduce(f32[768]{0:T(1024)S(1)} %get-tuple-element.30, ...), channel_id=6, replica_groups=mesh['dp'=8,'tensor'=4] {'dp','tensor'}, use_global_device_ids=true, to_apply=%region_19.20.clone | all-reduce | flops 9216 | bytes 73728
  492.3 31.4 %reduce-scatter.15.cloned.1.call-done = f32[96,768]{1,0:T(8,128)} async-done(((f32[768,768]{1,0:T(8,128)}), f32[96,768]{1,0:T(8,128)}) %reduce-scatter.15.cloned.1.call-update) | async-done | bytes 294928 | tf_op jit(solution)/shard_map/reduce_scatter | solution.py:56
  (181 shorter events, 63.3 us)
Async XLA Ops:
  8.0 90.7 %all-gather.7.cloned.1.call-start = ((), (), s32[]{:S(2)}) async-start(), calls=%async_computation.8 | async-start | bytes 1966080 | tf_op jit(solution)/shard_map/all_gather | solution.py:63
  10.5 51.4 %copy-start.10 = (f32[256]{0:T(256)}, f32[256]{0:T(256)S(1)}, u32[]{:S(2)}) copy-start(f32[256]{0:T(256)S(1)} %add_rsqrt_fusion.1) | copy-start | bytes 3076
  59.6 28.2 %copy-start.22 = (s32[1,2]{1,0:T(1,128)S(1)}, s32[1,2]{1,0:T(1,128)}, u32[]{:S(2)}) copy-start(s32[1,2]{1,0:T(1,128)} %param.16) | copy-start | bytes 28
  61.6 86.8 %reduce-scatter.7.cloned.1.call-start = ((), (), s32[]{:S(2)}) async-start(), calls=%async_computation.9 | async-start | bytes 1966080 | tf_op jit(solution)/shard_map/reduce_scatter | solution.py:67
  77.5 23.7 %copy-start.6 = (bf16[768,3,192]{0,2,1:T(8,128)(2,1)}, bf16[768,3,192]{0,2,1:T(8,128)(2,1)S(1)}, u32[]{:S(2)}) copy-start(bf16[768,3,192]{0,2,1:T(8,128)(2,1)S(1)} %copy.32) | copy-start | bytes 2654212
  111.6 36.8 %copy-start.2 = (bf16[256,768]{1,0:T(8,128)(2,1)S(1)}, bf16[256,768]{1,0:T(8,128)(2,1)}, u32[]{:S(2)}) copy-start(bf16[256,768]{1,0:T(8,128)(2,1)} %param.15) | copy-start | bytes 1179652
  114.2 40.4 %all-gather.11.cloned.1.call-start = ((), (), s32[]{:S(2)}) async-start(), calls=%async_computation.11 | async-start | bytes 1327104 | tf_op jit(solution)/shard_map/all_gather | solution.py:49
  114.7 74.2 %all-gather.9.cloned.1.call-start = ((), (), s32[]{:S(2)}) async-start(), calls=%async_computation.10 | async-start | bytes 1966080 | tf_op jit(solution)/shard_map/all_gather | solution.py:63
  152.9 60.5 %all-gather.13.cloned.1.call-start = ((), (), s32[]{:S(2)}) async-start(), calls=%async_computation.12 | async-start | bytes 1327104 | tf_op jit(solution)/shard_map/all_gather | solution.py:50
  153.5 98.5 %all-gather.15.cloned.1.call-start = ((), (), s32[]{:S(2)}) async-start(), calls=%async_computation.14 | async-start | bytes 1966080 | tf_op jit(solution)/shard_map/all_gather | solution.py:73
  154.3 142.2 %reduce-scatter.11.cloned.1.call-start = ((), (), s32[]{:S(2)}) async-start(), calls=%async_computation.15 | async-start | bytes 1966080 | tf_op jit(solution)/shard_map/reduce_scatter | solution.py:77
  154.6 107.7 %copy-start.17 = (f32[768]{0:T(1024)}, f32[768]{0:T(1024)S(1)}, u32[]{:S(2)}) copy-start(f32[768]{0:T(1024)S(1)} %dynamic-slice_convert_fusion) | copy-start | bytes 9220
  252.0 7.6 %copy-start.21 = (bf16[768,768]{1,0:T(8,128)(2,1)S(1)}, bf16[768,768]{1,0:T(8,128)(2,1)}, u32[]{:S(2)}) copy-start(bf16[768,768]{1,0:T(8,128)(2,1)} %all-gather.11.cloned.1.call-done) | copy-start | bytes 3538948
  262.2 34.3 %copy-start.3 = (bf16[256,768]{1,0:T(8,128)(2,1)S(1)}, bf16[256,768]{1,0:T(8,128)(2,1)}, u32[]{:S(2)}) copy-start(bf16[256,768]{1,0:T(8,128)(2,1)} %reduce-scatter.7.cloned.1.call-done) | copy-start | bytes 1179652
  262.2 70.7 %reduce-scatter.9.cloned.1.call-start = ((), (), s32[]{:S(2)}) async-start(), calls=%async_computation.13 | async-start | bytes 1966080 | tf_op jit(solution)/shard_map/reduce_scatter | solution.py:67
  267.9 104.7 %all-gather.17.cloned.1.call-start = ((), (), s32[]{:S(2)}) async-start(), calls=%async_computation.16 | async-start | bytes 1966080 | tf_op jit(solution)/shard_map/all_gather | solution.py:73
  336.5 107.9 %reduce-scatter.13.cloned.1.call-start = ((), (), s32[]{:S(2)}) async-start(), calls=%async_computation.17 | async-start | bytes 1966080 | tf_op jit(solution)/shard_map/reduce_scatter | solution.py:77
  372.5 7.0 %slice-start.2 = ((s8[6291456]{0:T(1024)(128)(4,1)}), s8[4194304]{0:T(1024)(128)(4,1)S(1)}, s32[]{:S(2)}) async-start(s8[6291456]{0:T(1024)(128)(4,1)} %bitcast.83), calls=%async_computation.22 | async-start | bytes 8388608
  379.5 6.3 %slice-start = ((s8[6291456]{0:T(1024)(128)(4,1)}), s8[4194304]{0:T(1024)(128)(4,1)S(1)}, s32[]{:S(2)}) async-start(s8[6291456]{0:T(1024)(128)(4,1)} %bitcast.81), calls=%async_computation.20 | async-start | bytes 8388608
  397.7 94.6 %reduce-scatter.17.cloned.1.call-start = ((), (), s32[]{:S(2)}) async-start(), calls=%async_computation.19 | async-start | bytes 2654208 | tf_op jit(solution)/shard_map/reduce_scatter | solution.py:57
  403.0 5.2 copy-start.5
  403.0 120.7 %reduce-scatter.15.cloned.1.call-start = ((), (), s32[]{:S(2)}) async-start(), calls=%async_computation.18 | async-start | bytes 2654208 | tf_op jit(solution)/shard_map/reduce_scatter | solution.py:56
  411.0 12.0 %all-to-all-start.1 = ((bf16[8,192,96]{2,1,0:T(8,128)(2,1)}), bf16[8,192,96]{2,1,0:T(8,128)(2,1)S(1)}, u32[]{:S(2)}, u32[]{:S(2)}) async-start(bf16[8,192,96]{2,1,0:T(8,128)(2,1)} %bitcast.79), calls=%async_computation.5 | async-start | bytes 786432 | tf_op jit(solution)/shard_map/all_to_all | solution.py:17
  417.4 9.2 %copy-start.16 = (f32[768]{0:T(1024)S(1)}, f32[768]{0:T(1024)}, u32[]{:S(2)}) copy-start(f32[768]{0:T(1024)} %get-tuple-element.52) | copy-start | bytes 9220
  417.4 9.5 %copy-start.19 = (f32[3,64]{1,0:T(4,128)S(1)}, f32[3,64]{1,0:T(4,128)}, u32[]{:S(2)}) copy-start(f32[3,64]{1,0:T(4,128)} %get-tuple-element.77) | copy-start | bytes 2308
  418.6 25.8 %copy-start.11 = (f32[256]{0:T(256)S(1)}, f32[256]{0:T(256)}, u32[]{:S(2)}) copy-start(f32[256]{0:T(256)} %copy-done.10) | copy-start | bytes 3076
  419.9 26.0 %copy-start.12 = (f32[768]{0:T(1024)S(1)}, f32[768]{0:T(1024)}, u32[]{:S(2)}) copy-start(f32[768]{0:T(1024)} %get-tuple-element.28) | copy-start | bytes 9220
  419.9 26.0 %copy-start.13 = (f32[768]{0:T(1024)S(1)}, f32[768]{0:T(1024)}, u32[]{:S(2)}) copy-start(f32[768]{0:T(1024)} %get-tuple-element.34) | copy-start | bytes 9220
  419.9 26.0 %copy-start.14 = (f32[768]{0:T(1024)S(1)}, f32[768]{0:T(1024)}, u32[]{:S(2)}) copy-start(f32[768]{0:T(1024)} %get-tuple-element.54) | copy-start | bytes 9220
  419.9 26.0 %copy-start.15 = (f32[768]{0:T(1024)S(1)}, f32[768]{0:T(1024)}, u32[]{:S(2)}) copy-start(f32[768]{0:T(1024)} %get-tuple-element.60) | copy-start | bytes 9220
  419.9 70.2 %copy-start.4 = (f32[256,768]{1,0:T(8,128)S(1)}, f32[256,768]{1,0:T(8,128)}, u32[]{:S(2)}) copy-start(f32[256,768]{1,0:T(8,128)} %get-tuple-element.56) | copy-start | bytes 2359300
  423.0 20.3 %all-to-all-start = ((bf16[8,96,3,192]{1,3,2,0:T(8,128)(2,1)}), bf16[8,96,3,192]{1,3,2,0:T(8,128)(2,1)S(1)}, u32[]{:S(2)}, u32[]{:S(2)}) async-start(bf16[8,96,3,192]{1,3,2,0:T(8,128)(2,1)} %copy.35), calls=%async_computation.4 | async-start | bytes 2359296 | tf_op jit(solution)/shard_map/all_to_all | solution.py:17
  (10 other events, 27.6 us)
Sparse Core Ops, SparseCore 0:
  61.7 36.9 all-gather.6
  114.3 34.1 reduce-scatter.6
  262.3 34.1 reduce-scatter.10
  298.7 34.2 reduce-scatter.8
Sparse Core Ops, SparseCore 1:
  116.5 22.7 all-gather.10
  153.0 35.9 all-gather.8
  190.7 22.7 all-gather.12
  215.1 36.9 all-gather.14
  336.6 35.9 all-gather.16
  397.8 34.1 reduce-scatter.12
  435.8 41.3 reduce-scatter.16
  481.3 42.4 reduce-scatter.14
where the time goes:
time: 536 us; the launch traced here: 531 us
  waiting for transfers between devices  286 us (53%)
  blocking collectives  105 us (20%)
  matrix products  64.9 us (12%)
  other arithmetic  28.4 us (5%)
  local copies, waits for them, and re-layouts  22.3 us (4%)
  between operations  16.4 us (3%)
  starting transfers between devices  8.17 us (2%)
    unnamed x2, blocking collectives  81.9 us
    all_gather x2, waiting for transfers between devices, rows_backward(): return lax.all_gather(values, 'tensor', axis=0, tiled=True)  74.5 us
    reduce_scatter x2, waiting for transfers between devices, sums_forward(): lax.psum_scatter(values.astype(jnp.bfloat16), 'tensor', scatter_dimension...  68 us
    all_gather x2, waiting for transfers between devices, rows_forward(): return lax.all_gather(values, 'tensor', axis=0, tiled=True)  44 us
    reduce_scatter x1, waiting for transfers between devices, scatter_ffn(): lax.psum_scatter(fc_grad, 'dp', scatter_dimension=0, tiled=True)  31.4 us
    reduce_scatter x2, waiting for transfers between devices, sums_backward(): lax.psum_scatter(values.astype(jnp.bfloat16), 'tensor', scatter_dimension...  28.6 us
    all_gather x1, waiting for transfers between devices, gather_ffn(): lax.all_gather(proj_weight, 'dp', axis=1, tiled=True)  19.7 us
    all_to_all x2, waiting for transfers between devices, sum_at_owner(): lax.all_to_all(blocks, axis, split_axis=0, concat_axis=0, tiled=True)  18.1 us
  transfers between devices with their start and end apart: 14, of which 11 were waited for; matrix products, arithmetic and copies ran while one was open for 9% of the time, Pallas kernels for 0%

commit v1 on v0

--- a/solution.py
+++ b/solution.py
@@ -2,6 +2,7 @@
 import jax.numpy as jnp
 from jax import lax
 from jax.sharding import PartitionSpec as P
+from jax.lax import axis_index, ppermute, psum
 
 HEAD_DIM = 64
 EPS = 1e-05
@@ -45,10 +46,20 @@
 
 
 def gather_ffn(fc_weight, proj_weight):
-    return (
-        lax.all_gather(fc_weight, "dp", axis=0, tiled=True),
-        lax.all_gather(proj_weight, "dp", axis=1, tiled=True),
-    )
+
+    def expand_roots(original):
+        ready = psum(1, "dp")
+        y_new = axis_index("dp")
+        h_now, found_now, block_now = (ready, y_new, original.shape[1])
+        built, back = (original, 1)
+        while back < h_now:
+            next_value = ppermute(built, "dp", [(jj, (jj - back) % h_now) for jj in range(h_now)])
+            built = jnp.concatenate([built, next_value], axis=1)
+            back = 2 * back
+        tmp = jnp.roll(built, found_now * block_now, axis=1)
+        return tmp
+
+    return (lax.all_gather(fc_weight, "dp", axis=0, tiled=True), expand_roots(proj_weight))
 
 
 def scatter_ffn(fc_grad, proj_grad):

time: 536 us -> 510 us (0.951)
  waiting for transfers between devices: 286 us -> 249 us
  other arithmetic: 28.4 us -> 35.9 us
    all_gather x2, waiting for transfers between devices: 44 us -> 9.6 us  [rows_forward(): return lax.all_gather(values, 'tensor', axis=0, tiled=True)]
    ppermute x0 -> x3, waiting for transfers between devices: none -> 26.2 us  [expand_roots(): ppermute(built, 'dp', [(jj, (jj - back) % h_now) for jj in range(h_now)])]
    all_gather x1 -> x0, waiting for transfers between devices: 19.7 us -> none  [gather_ffn(): lax.all_gather(proj_weight, 'dp', axis=1, tiled=True)]
    all_gather x2, waiting for transfers between devices: 74.5 us -> 66.3 us  [rows_backward(): return lax.all_gather(values, 'tensor', axis=0, tiled=True)]
    concatenate x0 -> x3, other arithmetic: none -> 7.29 us  [the longest x1 6.42 us: expand_roots(): tmp = jnp.roll(built, found_now * block_now, axis=1)]
    unnamed x83 -> x87, local copies, waits for them, and re-layouts: 16.4 us -> 17.2 us
  transfers between devices with their start and end apart: 14 -> 16, of which waited for: 11 -> 12; matrix products, arithmetic and copies ran while one was open for 9% -> 11% of each run, Pallas kernels for 0% -> 0%
where the time goes in v1:
time: 510 us; the launch traced here: 505 us
  waiting for transfers between devices  249 us (49%)
  blocking collectives  105 us (21%)
  matrix products  64.8 us (13%)
  other arithmetic  35.9 us (7%)
  local copies, waits for them, and re-layouts  23 us (5%)
  between operations  16.1 us (3%)
  starting transfers between devices  11.1 us (2%)
    unnamed x2, blocking collectives  81.9 us
    reduce_scatter x2, waiting for transfers between devices, sums_forward(): lax.psum_scatter(values.astype(jnp.bfloat16), 'tensor', scatter_dimension...  68 us
    all_gather x2, waiting for transfers between devices, rows_backward(): return lax.all_gather(values, 'tensor', axis=0, tiled=True)  66.3 us
    reduce_scatter x1, waiting for transfers between devices, scatter_ffn(): lax.psum_scatter(fc_grad, 'dp', scatter_dimension=0, tiled=True)  31.6 us
    reduce_scatter x2, waiting for transfers between devices, sums_backward(): lax.psum_scatter(values.astype(jnp.bfloat16), 'tensor', scatter_dimension...  28.6 us
    ppermute x3, waiting for transfers between devices, expand_roots(): ppermute(built, 'dp', [(jj, (jj - back) % h_now) for jj in range(h_now)])  26.2 us
    all_to_all x2, waiting for transfers between devices, sum_at_owner(): lax.all_to_all(blocks, axis, split_axis=0, concat_axis=0, tiled=True)  18.1 us
    unnamed x87, local copies, waits for them, and re-layouts  17.2 us
  transfers between devices with their start and end apart: 16, of which 12 were waited for; matrix products, arithmetic and copies ran while one was open for 11% of the time, Pallas kernels for 0%

profile of v1, /device:TPU:0, one launch (start us, length us, event | category | flops | bytes accessed | tf_op | source)
XLA Modules:
  0.0 505.5 jit_solution(907564977487804330)
XLA Ops:
  17.2 42.4 %all-reduce.17 = (bf16[1536]{0:T(1024)(128)(2,1)S(1)}, bf16[768]{0:T(1024)(128)(2,1)S(1)}, bf16[768]{0:T(1024)(128)(2,1)S(1)}, bf16[768]{0:T(1024)(128)(2,1)S(1)...) all-reduce(bf16[1536]{0:T(1024)(128)(2,1)S(1)} %dynamic-update-slic, ...), channel_id=1, replica_groups=mesh['dp'=8,'tensor'=4] {'dp','tensor'}, use_global_device_ids=true, to_apply=%add.2 | all-reduce | flops 9216 | bytes 36864
  63.8 12.9 %all_gather.51 = bf16[768,3,192]{2,1,0:T(4,128)(2,1)S(1)} all-gather(bf16[96,3,192]{2,1,0:T(4,128)(2,1)S(1)} %copy.32), channel_id=1, replica_groups=mesh['dp'=8,'tensor'=4] {'dp'}, dimensions={0}, use_global_device_ids=true | all-gather | bytes 995328 | tf_op jit(solution)/shard_map/all_gather | solution.py:43
  77.5 10.3 %all_gather.53 = bf16[192,768]{0,1:T(8,128)(2,1)S(1)} all-gather(bf16[192,96]{0,1:T(8,128)(2,1)S(1)} %copy.34), channel_id=1, replica_groups=mesh['dp'=8,'tensor'=4] {'dp'}, dimensions={1}, use_global_device_ids=true | all-gather | bytes 331776 | tf_op jit(solution)/shard_map/all_gather | solution.py:44
  89.1 9.6 %all-gather.6.cloned.1.call-done = bf16[1024,768]{1,0:T(8,128)(2,1)} async-done(((bf16[256,768]{1,0:T(8,128)(2,1)}), bf16[1024,768]{1,0:T(8,128)(2,1)}) %all-gather.6.cloned.1.call-update) | async-done | bytes 1572880 | tf_op jit(solution)/shard_map/all_gather | solution.py:74
  98.7 2.5 fusion.64
  114.8 33.6 %reduce-scatter.7.cloned.1.call-done = bf16[256,768]{1,0:T(8,128)(2,1)} async-done(((bf16[1024,768]{1,0:T(8,128)(2,1)}), bf16[256,768]{1,0:T(8,128)(2,1)}) %reduce-scatter.7.cloned.1.call-update) | async-done | bytes 393232 | tf_op jit(solution)/shard_map/reduce_scatter | solution.py:78
  155.3 2.7 collective-permute-done
  158.9 8.7 %collective-permute-done.1 = bf16[768,192]{0,1:T(8,128)(2,1)S(1)} collective-permute-done((bf16[768,192]{0,1:T(8,128)(2,1)S(1)}, bf16[768,192]{0,1:T(8,128)(2,1)S(1)}, u32[]{:S(2)}, u32[]{:S(2)}) %collective-permute-start.1) | collective-permute-done | bytes 294944 | tf_op jit(solution)/shard_map/ppermute | solution.py:56
  169.9 14.8 %collective-permute-done.2 = bf16[768,384]{0,1:T(8,128)(2,1)} collective-permute-done((bf16[768,384]{0,1:T(8,128)(2,1)}, bf16[768,384]{0,1:T(8,128)(2,1)}, u32[]{:S(2)}, u32[]{:S(2)}) %collective-permute-start.2) | collective-permute-done | bytes 589856 | tf_op jit(solution)/shard_map/ppermute | solution.py:56
  184.7 6.4 %fusion.24 = bf16[768,768]{0,1:T(8,128)(2,1)} fusion(s32[]{:T(128)S(6)} %select_n.37, bf16[768,96]{0,1:T(8,128)(2,1)S(1)} %copy-done.6, bf16[768,96]{0,1:T(8,128)(2,1)S(1)} %collective-permute-done, bf16[768,192]{0,1:T(8,128)(2,1)} %copy-done.7, bf16[768,384]{0,1:T(8,128)(2,1)} %collective-permute-done.2), kind=kLoop, calls=%fused_computation.70 | loop fusion | flops 9437184 | bytes 2359300 | tf_op jit(solution)/shard_map/jit(_roll_dynamic)/concatenate | solution.py:59
  191.1 4.8 fusion.65
  195.9 30.3 %all-gather.12.cloned.1.call-done = bf16[1024,768]{1,0:T(8,128)(2,1)} async-done(((bf16[256,768]{1,0:T(8,128)(2,1)}), bf16[1024,768]{1,0:T(8,128)(2,1)}) %all-gather.12.cloned.1.call-update) | async-done | bytes 1572880 | tf_op jit(solution)/shard_map/all_gather | solution.py:84
  226.2 6.4 %convert_reduce_fusion = (f32[768]{0:T(1024)}, bf16[1024,768]{1,0:T(8,128)(2,1)S(1)}) fusion(f32[1024,768]{1,0:T(8,128)} %fusion.65, f32[768]{0:T(1024)S(1)} %dynamic-slice_convert_fusion, bf16[1024,768]{1,0:T(8,128)(2,1)} %all-gather.12.cloned.1.call-done, bf16[768,768]{0,1:T(8,128)(2,1)} %fusion.24), kind=kOutput, calls=%fused_computation.29 | convolution fusion | flops 1226046720 | bytes 7477248 | tf_op jit(solution)/shard_map/id,fd->if/dot_general | solution.py:230
  233.8 2.6 convolution_convert_fusion
  236.5 5.6 %convolution_convert_fusion.1 = bf16[1024,768]{1,0:T(8,128)(2,1)} fusion(bf16[768,768]{0,1:T(8,128)(2,1)} %fusion.24, f32[1024,768]{1,0:T(8,128)} %fusion.65, f32[768]{0:T(1024)S(1)} %dynamic-slice_convert_fusion), kind=kOutput, calls=%fused_computation.45 | convolution fusion | flops 1216610304 | bytes 5901312 | tf_op jit(solution)/shard_map/dot_general | solution.py:222
  242.1 28.6 %reduce-scatter.11.cloned.1.call-done = bf16[256,768]{1,0:T(8,128)(2,1)} async-done(((bf16[1024,768]{1,0:T(8,128)(2,1)}), bf16[256,768]{1,0:T(8,128)(2,1)}) %reduce-scatter.11.cloned.1.call-update) | async-done | bytes 393232 | tf_op jit(solution)/shard_map/reduce_scatter | solution.py:88
  272.8 34.3 %reduce-scatter.9.cloned.1.call-done = bf16[256,768]{1,0:T(8,128)(2,1)} async-done(((bf16[1024,768]{1,0:T(8,128)(2,1)}), bf16[256,768]{1,0:T(8,128)(2,1)}) %reduce-scatter.9.cloned.1.call-update) | async-done | bytes 393232 | tf_op jit(solution)/shard_map/reduce_scatter | solution.py:78
  307.2 3.5 convert_reduce_fusion.6
  310.8 35.9 %all-gather.14.cloned.1.call-done = bf16[1024,768]{1,0:T(8,128)(2,1)} async-done(((bf16[256,768]{1,0:T(8,128)(2,1)}), bf16[1024,768]{1,0:T(8,128)(2,1)}) %all-gather.14.cloned.1.call-update) | async-done | bytes 1572880 | tf_op jit(solution)/shard_map/all_gather | solution.py:84
  349.0 4.7 fusion.57
  360.3 2.5 multiply_reduce_fusion
  362.8 2.6 convert_reduce_fusion.8
  369.5 2.6 bitcast_convert_fusion
  372.2 5.1 %fusion.60 = f32[768,768]{0,1:T(8,128)} fusion(bf16[1024,768]{1,0:T(8,128)(2,1)S(1)} %copy-done.22, f32[1024,768]{1,0:T(8,128)} %fusion.65, f32[768]{0:T(1024)S(1)} %copy-done.20), kind=kOutput, calls=%fused_computation.138 | convolution fusion | flops 1215823872 | bytes 7080960 | tf_op jit(solution)/shard_map/if,id->fd/dot_general | solution.py:229
  377.6 4.8 fusion.67
  385.2 3.7 all-to-all-start.1
  389.0 2.5 fusion.68
  394.2 3.0 all-to-all-done.1
  397.2 3.6 all-to-all-start
  402.5 15.1 %all-to-all-done = bf16[8,96,3,192]{1,3,2,0:T(8,128)(2,1)S(1)} async-done(((bf16[8,96,3,192]{1,3,2,0:T(8,128)(2,1)}), bf16[8,96,3,192]{1,3,2,0:T(8,128)(2,1)S(1)}, u32[]{:S(2)}, u32[]{:S(2)}) %all-to-all-start) | async-done | bytes 884768 | tf_op jit(solution)/shard_map/all_to_all | solution.py:18
  420.2 39.5 %all-reduce.16 = (f32[768]{0:T(1024)S(1)}, f32[768]{0:T(1024)S(1)}, f32[1536]{0:T(1024)S(1)}, f32[768]{0:T(1024)S(1)}, f32[768]{0:T(1024)S(1)}, /*index=5*/f32[7...) all-reduce(f32[768]{0:T(1024)S(1)} %get-tuple-element.31, ...), channel_id=6, replica_groups=mesh['dp'=8,'tensor'=4] {'dp','tensor'}, use_global_device_ids=true, to_apply=%region_19.21.clone | all-reduce | flops 9216 | bytes 73728
  466.6 31.6 %reduce-scatter.15.cloned.1.call-done = f32[96,768]{1,0:T(8,128)} async-done(((f32[768,768]{1,0:T(8,128)}), f32[96,768]{1,0:T(8,128)}) %reduce-scatter.15.cloned.1.call-update) | async-done | bytes 294928 | tf_op jit(solution)/shard_map/reduce_scatter | solution.py:67
  (191 shorter events, 72.1 us)
Async XLA Ops:
  8.0 90.7 %all-gather.6.cloned.1.call-start = ((), (), s32[]{:S(2)}) async-start(), calls=%async_computation.8 | async-start | bytes 1966080 | tf_op jit(solution)/shard_map/all_gather | solution.py:74
  10.5 51.4 %copy-start.12 = (f32[256]{0:T(256)}, f32[256]{0:T(256)S(1)}, u32[]{:S(2)}) copy-start(f32[256]{0:T(256)S(1)} %add_rsqrt_fusion.1) | copy-start | bytes 3076
  59.6 28.2 %copy-start.24 = (s32[1,2]{1,0:T(1,128)S(1)}, s32[1,2]{1,0:T(1,128)}, u32[]{:S(2)}) copy-start(s32[1,2]{1,0:T(1,128)} %param.18) | copy-start | bytes 28
  61.6 86.8 %reduce-scatter.7.cloned.1.call-start = ((), (), s32[]{:S(2)}) async-start(), calls=%async_computation.9 | async-start | bytes 1966080 | tf_op jit(solution)/shard_map/reduce_scatter | solution.py:78
  77.5 23.7 %copy-start.8 = (bf16[768,3,192]{0,2,1:T(8,128)(2,1)}, bf16[768,3,192]{0,2,1:T(8,128)(2,1)S(1)}, u32[]{:S(2)}) copy-start(bf16[768,3,192]{0,2,1:T(8,128)(2,1)S(1)} %copy.33) | copy-start | bytes 2654212
  111.6 36.8 %copy-start.2 = (bf16[256,768]{1,0:T(8,128)(2,1)S(1)}, bf16[256,768]{1,0:T(8,128)(2,1)}, u32[]{:S(2)}) copy-start(bf16[256,768]{1,0:T(8,128)(2,1)} %param.17) | copy-start | bytes 1179652
  114.1 39.4 %copy-start.6 = (bf16[768,96]{0,1:T(8,128)(2,1)S(1)}, bf16[768,96]{0,1:T(8,128)(2,1)}, u32[]{:S(2)}) copy-start(bf16[768,96]{0,1:T(8,128)(2,1)} %param.29) | copy-start | bytes 442372
  114.2 76.9 %all-gather.10.cloned.1.call-start = ((), (), s32[]{:S(2)}) async-start(), calls=%async_computation.11 | async-start | bytes 1327104 | tf_op jit(solution)/shard_map/all_gather | solution.py:62
  114.7 76.3 %all-gather.8.cloned.1.call-start = ((), (), s32[]{:S(2)}) async-start(), calls=%async_computation.10 | async-start | bytes 1966080 | tf_op jit(solution)/shard_map/all_gather | solution.py:74
  152.9 73.3 %all-gather.12.cloned.1.call-start = ((), (), s32[]{:S(2)}) async-start(), calls=%async_computation.13 | async-start | bytes 1966080 | tf_op jit(solution)/shard_map/all_gather | solution.py:84
  153.5 117.2 %reduce-scatter.11.cloned.1.call-start = ((), (), s32[]{:S(2)}) async-start(), calls=%async_computation.14 | async-start | bytes 1966080 | tf_op jit(solution)/shard_map/reduce_scatter | solution.py:88
  153.6 4.4 collective-permute-start
  158.0 9.7 %collective-permute-start.1 = (bf16[768,192]{0,1:T(8,128)(2,1)S(1)}, bf16[768,192]{0,1:T(8,128)(2,1)S(1)}, u32[]{:S(2)}, u32[]{:S(2)}) collective-permute-start(bf16[768,192]{0,1:T(8,128)(2,1)S(1)} %pad_maximum_fusion.3), channel_id=1, source_target_pairs={{0,24},{4,28},{8,0},{12,4},{16,8},{20,12},{24,16},{28,20},{1,25},{... | collective-permute-start | bytes 884744 | tf_op jit(solution)/shard_map/ppermute | solution.py:56
  169.2 15.4 %collective-permute-start.2 = (bf16[768,384]{0,1:T(8,128)(2,1)}, bf16[768,384]{0,1:T(8,128)(2,1)}, u32[]{:S(2)}, u32[]{:S(2)}) collective-permute-start(bf16[768,384]{0,1:T(8,128)(2,1)} %pad_maximum_fusion.1), channel_id=1, source_target_pairs={{0,16},{4,20},{8,24},{12,28},{16,0},{20,4},{24,8},{28,12},{1,17},{... | collective-permute-start | bytes 1769480 | tf_op jit(solution)/shard_map/ppermute | solution.py:56
  169.9 66.6 %copy-start.19 = (f32[768]{0:T(1024)}, f32[768]{0:T(1024)S(1)}, u32[]{:S(2)}) copy-start(f32[768]{0:T(1024)S(1)} %dynamic-slice_convert_fusion) | copy-start | bytes 9220
  226.2 7.6 %copy-start.23 = (bf16[768,768]{1,0:T(8,128)(2,1)S(1)}, bf16[768,768]{1,0:T(8,128)(2,1)}, u32[]{:S(2)}) copy-start(bf16[768,768]{1,0:T(8,128)(2,1)} %all-gather.10.cloned.1.call-done) | copy-start | bytes 3538948
  236.4 34.3 %copy-start.3 = (bf16[256,768]{1,0:T(8,128)(2,1)S(1)}, bf16[256,768]{1,0:T(8,128)(2,1)}, u32[]{:S(2)}) copy-start(bf16[256,768]{1,0:T(8,128)(2,1)} %reduce-scatter.7.cloned.1.call-done) | copy-start | bytes 1179652
  236.4 70.8 %reduce-scatter.9.cloned.1.call-start = ((), (), s32[]{:S(2)}) async-start(), calls=%async_computation.12 | async-start | bytes 1966080 | tf_op jit(solution)/shard_map/reduce_scatter | solution.py:78
  242.0 104.7 %all-gather.14.cloned.1.call-start = ((), (), s32[]{:S(2)}) async-start(), calls=%async_computation.15 | async-start | bytes 1966080 | tf_op jit(solution)/shard_map/all_gather | solution.py:84
  310.7 108.0 %reduce-scatter.13.cloned.1.call-start = ((), (), s32[]{:S(2)}) async-start(), calls=%async_computation.16 | async-start | bytes 1966080 | tf_op jit(solution)/shard_map/reduce_scatter | solution.py:88
  372.1 94.5 %reduce-scatter.17.cloned.1.call-start = ((), (), s32[]{:S(2)}) async-start(), calls=%async_computation.18 | async-start | bytes 2654208 | tf_op jit(solution)/shard_map/reduce_scatter | solution.py:68
  377.3 120.8 %reduce-scatter.15.cloned.1.call-start = ((), (), s32[]{:S(2)}) async-start(), calls=%async_computation.17 | async-start | bytes 2654208 | tf_op jit(solution)/shard_map/reduce_scatter | solution.py:67
  385.2 12.0 %all-to-all-start.1 = ((bf16[8,192,96]{2,1,0:T(8,128)(2,1)}), bf16[8,192,96]{2,1,0:T(8,128)(2,1)S(1)}, u32[]{:S(2)}, u32[]{:S(2)}) async-start(bf16[8,192,96]{2,1,0:T(8,128)(2,1)} %bitcast.92), calls=%async_computation.5 | async-start | bytes 786432 | tf_op jit(solution)/shard_map/all_to_all | solution.py:18
  391.6 9.2 %copy-start.18 = (f32[768]{0:T(1024)S(1)}, f32[768]{0:T(1024)}, u32[]{:S(2)}) copy-start(f32[768]{0:T(1024)} %get-tuple-element.78) | copy-start | bytes 9220
  391.7 9.5 %copy-start.21 = (f32[3,64]{1,0:T(4,128)S(1)}, f32[3,64]{1,0:T(4,128)}, u32[]{:S(2)}) copy-start(f32[3,64]{1,0:T(4,128)} %get-tuple-element.76) | copy-start | bytes 2308
  392.9 25.8 %copy-start.13 = (f32[256]{0:T(256)S(1)}, f32[256]{0:T(256)}, u32[]{:S(2)}) copy-start(f32[256]{0:T(256)} %copy-done.12) | copy-start | bytes 3076
  394.2 26.0 %copy-start.14 = (f32[768]{0:T(1024)S(1)}, f32[768]{0:T(1024)}, u32[]{:S(2)}) copy-start(f32[768]{0:T(1024)} %get-tuple-element.29) | copy-start | bytes 9220
  394.2 26.0 %copy-start.15 = (f32[768]{0:T(1024)S(1)}, f32[768]{0:T(1024)}, u32[]{:S(2)}) copy-start(f32[768]{0:T(1024)} %get-tuple-element.35) | copy-start | bytes 9220
  394.2 26.0 %copy-start.16 = (f32[768]{0:T(1024)S(1)}, f32[768]{0:T(1024)}, u32[]{:S(2)}) copy-start(f32[768]{0:T(1024)} %get-tuple-element.53) | copy-start | bytes 9220
  394.2 26.0 %copy-start.17 = (f32[768]{0:T(1024)S(1)}, f32[768]{0:T(1024)}, u32[]{:S(2)}) copy-start(f32[768]{0:T(1024)} %get-tuple-element.59) | copy-start | bytes 9220
  394.2 70.2 %copy-start.4 = (f32[256,768]{1,0:T(8,128)S(1)}, f32[256,768]{1,0:T(8,128)}, u32[]{:S(2)}) copy-start(f32[256,768]{1,0:T(8,128)} %get-tuple-element.55) | copy-start | bytes 2359300
  397.2 20.3 %all-to-all-start = ((bf16[8,96,3,192]{1,3,2,0:T(8,128)(2,1)}), bf16[8,96,3,192]{1,3,2,0:T(8,128)(2,1)S(1)}, u32[]{:S(2)}, u32[]{:S(2)}) async-start(bf16[8,96,3,192]{1,3,2,0:T(8,128)(2,1)} %copy.37), calls=%async_computation.4 | async-start | bytes 2359296 | tf_op jit(solution)/shard_map/all_to_all | solution.py:18
  (14 other events, 47.2 us)
Sparse Core Ops, SparseCore 0:
  61.7 36.9 all-gather.5
  114.3 34.1 reduce-scatter.6
  236.5 34.1 reduce-scatter.10
  272.9 34.2 reduce-scatter.8
Sparse Core Ops, SparseCore 1:
  116.5 22.7 all-gather.9
  153.0 35.9 all-gather.7
  190.4 35.8 all-gather.11
  310.8 35.9 all-gather.13
  372.2 34.1 reduce-scatter.12
  410.3 41.3 reduce-scatter.16
  455.8 42.3 reduce-scatter.14
